TPU v7x, 32 devices: a whole 2x2x4 slice. The times are simulated.
32 devices in a mesh: cells: 4 (over y, x), genes: 8 (over z, core).
Axes of the slice: x: 2, y: 2, z: 4, core: 2. Of those that a mesh axis runs over, the one named last changes fastest.
Arguments:
- counts: bfloat16 [32768, 2560], P('cells', 'genes'), may hold values from 0 to 8, as said below
- library: float32 [32768], P('cells'), may hold values from 7 to 10
- noise: float32 [32768, 10], P('cells'), may hold values from -4 to 4
- batch_ids: int32 [32768], P('cells'), may hold values from 0 to 127
- gene_mask: int32 [2560], P('genes'), may hold values 0 or 1
- kl_weight: float32 [1], replicated, may hold values from 0.5 to 1
- enc_w: float32 [2560, 128], P('genes'), may hold values from -0.125 to 0.125
- enc_m: float32 [2560, 128], P('genes'), may hold values from -6.1035156e-05 to 6.1035156e-05
- enc_v: float32 [2560, 128], P('genes'), may hold values from 1.0172526e-11 to 4.0690104e-11
- dec_w: float32 [2, 128, 2560], P(None, None, 'genes'), may hold values from -0.5 to 0.5
- dec_m: float32 [2, 128, 2560], P(None, None, 'genes'), may hold values from -6.1035156e-05 to 6.1035156e-05
- dec_v: float32 [2, 128, 2560], P(None, None, 'genes'), may hold values from 1.0172526e-11 to 4.0690104e-11
- gene_par: float32 [3, 2560], P(None, 'genes'), may hold values from -3 to 3
- gene_m: float32 [3, 2560], P(None, 'genes'), may hold values from -0.00024414062 to 0.00024414062
- gene_v: float32 [3, 2560], P(None, 'genes'), may hold values from 1.6276042e-10 to 6.5104167e-10
- small_w: float32 [266, 128], replicated, may hold values from -3 to 3
- small_m: float32 [266, 128], replicated, may hold values from -3.0517578e-05 to 3.0517578e-05
- small_v: float32 [266, 128], replicated, may hold values from 3.0517578e-12 to 1.2207031e-11
- head_w: float32 [129, 20], replicated, may hold values from -0.5 to 0.5
- head_m: float32 [129, 20], replicated, may hold values from -0.00024414062 to 0.00024414062
- head_v: float32 [129, 20], replicated, may hold values from 1.6276042e-10 to 6.5104167e-10
- norm_par: float32 [4, 128], replicated, may hold values from 0.5 to 1.5
- norm_m: float32 [4, 128], replicated, may hold values from -0.00024414062 to 0.00024414062
- norm_v: float32 [4, 128], replicated, may hold values from 1.6276042e-10 to 6.5104167e-10
Outputs:
- enc_new: float32 [2560, 128], P('genes')
- enc_m_new: float32 [2560, 128], P('genes')
- enc_v_new: float32 [2560, 128], P('genes')
- enc_low: bfloat16 [2560, 128], P('genes')
- dec_new: float32 [2, 128, 2560], P(None, None, 'genes')
- dec_m_new: float32 [2, 128, 2560], P(None, None, 'genes')
- dec_v_new: float32 [2, 128, 2560], P(None, None, 'genes')
- dec_low: bfloat16 [2, 128, 2560], P(None, None, 'genes')
- gene_new: float32 [3, 2560], P(None, 'genes')
- gene_m_new: float32 [3, 2560], P(None, 'genes')
- gene_v_new: float32 [3, 2560], P(None, 'genes')
- small_new: float32 [266, 128], replicated
- small_m_new: float32 [266, 128], replicated
- small_v_new: float32 [266, 128], replicated
- head_new: float32 [129, 20], replicated
- head_m_new: float32 [129, 20], replicated
- head_v_new: float32 [129, 20], replicated
- norm_new: float32 [4, 128], replicated
- norm_m_new: float32 [4, 128], replicated
- norm_v_new: float32 [4, 128], replicated
- grad_norm: float32 [], replicated
- loss: float32 [32768], P(('cells', 'genes'))
Inputs may be any that keep to these rules, and one draw needn't show every extreme that they name: `counts`: whole numbers.
All inputs are finite; a program needn't handle non-finite values. No bound on the sum of `gene_mask` on one device may be relied on, other than what follows from the above.
Results may differ from a plain program's by a relative error of at most 0.0047.
Values may be sent and summed in bfloat16 or wider, within the bound.
No kernel may reach another device: no remote copies, remote signals or barrier semaphores. Data moves between devices by JAX's collectives and lax.ppermute only.
A program may use at most 192 MiB of HBM per device.

v0:
```python
import jax
import jax.numpy as jnp
from jax import lax
from jax.sharding import PartitionSpec as P

norm_epsilon = 0.001
zinb_epsilon = 1e-08
beta_one = 0.9
beta_two = 0.999
step_number = 5.0
decay_rate = 0.01
rate_genes = 0.03
rate_small = 0.2
max_norm = 0.1


def exact_dot(left, right):
    return jnp.dot(left, right, precision=lax.Precision.HIGHEST, preferred_element_type=jnp.float32)


def exact_inner(left, right):
    return lax.dot_general(
        left,
        right,
        (((0,), (0,)), ((), ())),
        precision=lax.Precision.HIGHEST,
        preferred_element_type=jnp.float32,
    )


def exact_back(left, right):
    return lax.dot_general(
        left,
        right,
        (((1,), (1,)), ((), ())),
        precision=lax.Precision.HIGHEST,
        preferred_element_type=jnp.float32,
    )


def plain_inner(left, right):
    return lax.dot_general(
        left, right, (((0,), (0,)), ((), ())), preferred_element_type=jnp.float32
    )


def plain_back(left, right):
    return lax.dot_general(
        left, right, (((1,), (1,)), ((), ())), preferred_element_type=jnp.float32
    )


def zinb_loglik(observed, log_mean, drop_logit, log_disp):
    dispersion = jnp.exp(log_disp)
    mean_rate = jnp.exp(log_mean)
    soft_drop = jax.nn.softplus(-drop_logit)
    log_disp_eps = jnp.log(dispersion + zinb_epsilon)
    log_both = jnp.log(dispersion + mean_rate + zinb_epsilon)
    drop_term = -drop_logit + dispersion * (log_disp_eps - log_both)
    case_zero = jax.nn.softplus(drop_term) - soft_drop
    case_other = (
        -soft_drop
        + drop_term
        + observed * (jnp.log(mean_rate + zinb_epsilon) - log_both)
        + lax.lgamma(observed + dispersion)
        - lax.lgamma(dispersion)
        - lax.lgamma(observed + 1.0)
    )
    return jnp.where(observed < zinb_epsilon, case_zero, case_other)


def wide_sum(values):
    return lax.psum((values[0], values[1]), ("cells", "genes"))


def norm_forward(pre_act, gain_row, shift_row, cell_total):
    stat_sums = wide_sum((jnp.sum(pre_act, 0), jnp.sum(pre_act * pre_act, 0)))
    stat_mean = stat_sums[0] / cell_total
    stat_var = stat_sums[1] / cell_total - stat_mean * stat_mean
    inv_std = lax.rsqrt(stat_var + norm_epsilon)
    centred = (pre_act - stat_mean) * inv_std
    affine = gain_row * centred + shift_row
    return (jax.nn.relu(affine), (centred, inv_std, affine > 0))


def norm_backward(gradient, saved, gain_row, cell_total):
    centred, inv_std, active = saved
    grad_affine = jnp.where(active, gradient, 0.0)
    stat_sums = wide_sum((jnp.sum(grad_affine, 0), jnp.sum(grad_affine * centred, 0)))
    grad_pre = (
        gain_row
        * inv_std
        * (grad_affine - stat_sums[0] / cell_total - centred * stat_sums[1] / cell_total)
    )
    return (grad_pre, stat_sums[1], stat_sums[0])


def adamw(weight, gradient, moment_one, moment_two, step_rate):
    moment_one = beta_one * moment_one + (1.0 - beta_one) * gradient
    moment_two = beta_two * moment_two + (1.0 - beta_two) * gradient * gradient
    fixed_one = moment_one / (1.0 - beta_one**step_number)
    fixed_two = moment_two / (1.0 - beta_two**step_number)
    update = fixed_one / (jnp.sqrt(fixed_two) + 1e-08) + decay_rate * weight
    return (weight - step_rate * update, moment_one, moment_two)


def per_device(
    counts,
    library,
    noise,
    batch_ids,
    gene_mask,
    kl_weight,
    enc_w,
    enc_m,
    enc_v,
    dec_w,
    dec_m,
    dec_v,
    gene_par,
    gene_m,
    gene_v,
    small_w,
    small_m,
    small_v,
    head_w,
    head_m,
    head_v,
    norm_par,
    norm_m,
    norm_v,
):
    rows_all = counts.shape[0]
    local_genes = counts.shape[1]
    cell_total = rows_all * lax.axis_size("cells")
    groups = lax.axis_size("genes")
    hidden = enc_w.shape[1]
    latent = head_w.shape[1] // 2
    batch_kinds = (small_w.shape[0] - latent) // 2
    log_counts = jnp.log1p(counts.astype(jnp.float32)).astype(jnp.bfloat16)
    enc_low = enc_w.astype(jnp.bfloat16)
    dec_cat = jnp.concatenate([dec_w[0], dec_w[1]], axis=1).astype(jnp.bfloat16)
    gene_keep = gene_mask > 0
    share_rows = rows_all // groups
    first_row = lax.axis_index("genes") * share_rows
    cell_rows = log_counts
    enc_part = lax.psum_scatter(
        jnp.dot(cell_rows, enc_low, preferred_element_type=jnp.float32),
        "genes",
        scatter_dimension=0,
        tiled=True,
    )
    own_batch = lax.dynamic_slice_in_dim(batch_ids, first_row, share_rows, 0)
    own_noise = lax.dynamic_slice_in_dim(noise, first_row, share_rows, 0)
    batch_table = (own_batch[:, None] == jnp.arange(batch_kinds, dtype=jnp.int32)[None, :]).astype(
        jnp.float32
    )
    pre_enc = enc_part + exact_dot(batch_table, small_w[:batch_kinds])
    hidden_enc, saved_enc = norm_forward(pre_enc, norm_par[0], norm_par[1], cell_total)
    head_out = exact_dot(hidden_enc, head_w[:hidden]) + head_w[hidden]
    latent_mean = head_out[:, :latent]
    latent_logvar = head_out[:, latent:]
    spread = jnp.exp(latent_logvar)
    latent_var = spread + 0.0001
    latent_std = jnp.sqrt(latent_var)
    latent_draw = latent_mean + latent_std * own_noise
    pre_dec = exact_dot(latent_draw, small_w[2 * batch_kinds :]) + exact_dot(
        batch_table, small_w[batch_kinds : 2 * batch_kinds]
    )
    hidden_dec, saved_dec = norm_forward(pre_dec, norm_par[2], norm_par[3], cell_total)
    hidden_low = hidden_dec.astype(jnp.bfloat16)
    hidden_all = lax.all_gather(hidden_low, "genes", axis=0, tiled=True)
    logits = jnp.dot(hidden_all, dec_cat, preferred_element_type=jnp.float32)
    score = logits[:, :local_genes] + gene_par[0]
    drop_logit = logits[:, local_genes:] + gene_par[1]
    masked = jnp.where(gene_keep, score, -1e30)
    local_top = jnp.max(masked, axis=1)
    top_logit = lax.pmax(local_top.astype(jnp.bfloat16), "genes").astype(local_top.dtype)
    local_mass = jnp.sum(jnp.where(gene_keep, jnp.exp(masked - top_logit[:, None]), 0.0), 1)
    exp_mass = lax.psum(local_mass, "genes")
    log_total = top_logit + jnp.log(exp_mass)
    log_mean = library[:, None] + score - log_total[:, None]
    block_rows = min(2048, rows_all)
    count_blocks = rows_all // block_rows
    disp_row = gene_par[2]

    def block_grad(block_args):
        block_counts, block_mean, block_drop = block_args

        def local_loss(mean_part, drop_part, disp_part):
            terms = zinb_loglik(block_counts.astype(jnp.float32), mean_part, drop_part, disp_part)
            return jnp.sum(jnp.where(gene_keep, terms, 0.0), axis=1)

        block_value, pullback = jax.vjp(local_loss, block_mean, block_drop, disp_row)
        grad_mean, grad_drop, grad_disp = pullback(
            jnp.full((block_counts.shape[0],), -1.0 / cell_total, jnp.float32)
        )
        return (block_value, grad_mean, grad_drop, grad_disp)

    block_values, grad_mean, grad_drop, grad_disp = lax.map(
        block_grad,
        (
            counts.reshape(count_blocks, block_rows, local_genes),
            log_mean.reshape(count_blocks, block_rows, local_genes),
            drop_logit.reshape(count_blocks, block_rows, local_genes),
        ),
    )
    recon_rows = block_values.reshape(rows_all)
    grad_mean = grad_mean.reshape(rows_all, local_genes)
    grad_drop = grad_drop.reshape(rows_all, local_genes)
    softmax_ratio = jnp.where(gene_keep, jnp.exp(score - log_total[:, None]), 0.0)
    back_mass, recon_cells = lax.psum((jnp.sum(grad_mean, 1), recon_rows), "genes")
    grad_score = grad_mean - softmax_ratio * back_mass[:, None]
    grad_cat = jnp.concatenate([grad_score, grad_drop], axis=1).astype(jnp.bfloat16)
    grad_dec = plain_inner(hidden_all, grad_cat)
    grad_gene = jnp.stack([jnp.sum(grad_score, 0), jnp.sum(grad_drop, 0), jnp.sum(grad_disp, 0)])
    cell_rows = grad_cat
    grad_hidden = lax.psum_scatter(
        plain_back(cell_rows, dec_cat), "genes", scatter_dimension=0, tiled=True
    )
    grad_pre_dec, gain_dec, shift_dec = norm_backward(
        grad_hidden, saved_dec, norm_par[2], cell_total
    )
    grad_latent_w = exact_inner(latent_draw, grad_pre_dec)
    grad_cov_dec = exact_inner(batch_table, grad_pre_dec)
    grad_draw = exact_back(grad_pre_dec, small_w[2 * batch_kinds :])
    kl_scale = kl_weight[0] / cell_total
    grad_lmean = grad_draw + kl_scale * latent_mean
    grad_lvar = grad_draw * own_noise * 0.5 * spread / latent_std + kl_scale * 0.5 * (
        spread - spread / latent_var
    )
    grad_head_out = jnp.concatenate([grad_lmean, grad_lvar], axis=1)
    grad_head = jnp.concatenate(
        [exact_inner(hidden_enc, grad_head_out), jnp.sum(grad_head_out, 0)[None, :]], axis=0
    )
    grad_hidden_enc = exact_back(grad_head_out, head_w[:hidden])
    grad_pre_enc, gain_enc, shift_enc = norm_backward(
        grad_hidden_enc, saved_enc, norm_par[0], cell_total
    )
    grad_cov_enc = exact_inner(batch_table, grad_pre_enc)
    grad_small = jnp.concatenate([grad_cov_enc, grad_cov_dec, grad_latent_w], axis=0)
    grad_norm_par = jnp.stack([gain_enc, shift_enc, gain_dec, shift_dec])
    grad_pre_low = grad_pre_enc.astype(jnp.bfloat16)
    diverge_rows = 0.5 * jnp.sum(
        latent_var + latent_mean * latent_mean - 1.0 - jnp.log(latent_var), axis=1
    )
    cell_rows = log_counts
    grad_enc = plain_inner(cell_rows, lax.all_gather(grad_pre_low, "genes", axis=0, tiled=True))
    grad_enc, grad_dec, grad_gene = lax.psum((grad_enc, grad_dec, grad_gene), "cells")
    grad_small, grad_head = lax.psum((grad_small, grad_head), ("cells", "genes"))
    own_recon = lax.dynamic_slice_in_dim(recon_cells, first_row, share_rows, 0)
    cell_loss = kl_weight[0] * diverge_rows - own_recon
    gene_square = (
        jnp.sum(grad_enc * grad_enc) + jnp.sum(grad_dec * grad_dec) + jnp.sum(grad_gene * grad_gene)
    )
    gene_square = lax.psum(gene_square, "genes")
    small_square = (
        jnp.sum(grad_small * grad_small)
        + jnp.sum(grad_head * grad_head)
        + jnp.sum(grad_norm_par * grad_norm_par)
    )
    norm_value = jnp.sqrt(gene_square + small_square)
    factor = jnp.minimum(1.0, max_norm / norm_value)
    grad_dec_split = jnp.stack([grad_dec[:, :local_genes], grad_dec[:, local_genes:]])
    enc_res = adamw(enc_w, grad_enc * factor, enc_m, enc_v, rate_genes)
    dec_res = adamw(dec_w, grad_dec_split * factor, dec_m, dec_v, rate_genes)
    gene_res = adamw(gene_par, grad_gene * factor, gene_m, gene_v, rate_small)
    small_res = adamw(small_w, grad_small * factor, small_m, small_v, rate_small)
    head_res = adamw(head_w, grad_head * factor, head_m, head_v, rate_small)
    norm_res = adamw(norm_par, grad_norm_par * factor, norm_m, norm_v, rate_small)
    return (
        enc_res[0],
        enc_res[1],
        enc_res[2],
        enc_res[0].astype(jnp.bfloat16),
        dec_res[0],
        dec_res[1],
        dec_res[2],
        dec_res[0].astype(jnp.bfloat16),
        gene_res[0],
        gene_res[1],
        gene_res[2],
        small_res[0],
        small_res[1],
        small_res[2],
        head_res[0],
        head_res[1],
        head_res[2],
        norm_res[0],
        norm_res[1],
        norm_res[2],
        norm_value,
        cell_loss,
    )


def solution(mesh):
    placed = (
        P("cells", "genes"),
        P("cells"),
        P("cells", None),
        P("cells"),
        P("genes"),
        P(),
        P("genes", None),
        P("genes", None),
        P("genes", None),
        P(None, None, "genes"),
        P(None, None, "genes"),
        P(None, None, "genes"),
        P(None, "genes"),
        P(None, "genes"),
        P(None, "genes"),
        P(),
        P(),
        P(),
        P(),
        P(),
        P(),
        P(),
        P(),
        P(),
    )
    return jax.shard_map(
        per_device,
        mesh=mesh,
        in_specs=placed,
        out_specs=(
            P("genes", None),
            P("genes", None),
            P("genes", None),
            P("genes", None),
            P(None, None, "genes"),
            P(None, None, "genes"),
            P(None, None, "genes"),
            P(None, None, "genes"),
            P(None, "genes"),
            P(None, "genes"),
            P(None, "genes"),
            P(),
            P(),
            P(),
            P(),
            P(),
            P(),
            P(),
            P(),
            P(),
            P(),
            P(("cells", "genes")),
        ),
        check_vma=False,
    )
```

profile of v0, /device:TPU:0, one launch (start us, length us, event | category | flops | bytes accessed | tf_op | source)
XLA Modules:
  0.0 1099.5 jit_solution(12833105348551881705)
XLA Ops:
  7.2 8.7 fusion.89
  16.9 51.9 %reduce-scatter.3.cloned.1.call-done = f32[1024,128]{1,0:T(8,128)} async-done(((f32[8192,128]{1,0:T(8,128)}), f32[1024,128]{1,0:T(8,128)}) %reduce-scatter.3.cloned.1.call-update) | async-done | bytes 524304 | tf_op jit(solution)/shard_map/reduce_scatter | solution.py:147
  70.3 37.8 %all-reduce.3 = (f32[128]{0:T(128)S(1)}, f32[128]{0:T(128)S(1)}) all-reduce(f32[128]{0:T(128)S(1)} %get-tuple-element.381, f32[128]{0:T(128)S(1)} %get-tuple-element.380), channel_id=1, replica_groups=mesh['cells'=4,'genes'=8] {'cells','genes'}, use_global_device_ids=true, to_apply=%region_2.0 | all-reduce | flops 256 | bytes 2048 | tf_op jit(solution)/shard_map/psum | solution.py:73
  112.4 41.4 %all-reduce.2 = (f32[128]{0:T(128)S(1)}, f32[128]{0:T(128)S(1)}) all-reduce(f32[128]{0:T(128)S(1)} %get-tuple-element.379, f32[128]{0:T(128)S(1)} %get-tuple-element.378), channel_id=1, replica_groups=mesh['cells'=4,'genes'=8] {'cells','genes'}, use_global_device_ids=true, to_apply=%region_6.7 | all-reduce | flops 256 | bytes 2048 | tf_op jit(solution)/shard_map/psum | solution.py:73
  155.5 8.2 copy.60
  163.9 20.5 %all-gather.3.cloned.1.call-done = bf16[8192,128]{1,0:T(8,128)(2,1)} async-done(((bf16[1024,128]{1,0:T(8,128)(2,1)}), bf16[8192,128]{1,0:T(8,128)(2,1)}) %all-gather.3.cloned.1.call-update) | async-done | bytes 2097168 | tf_op jit(solution)/shard_map/all_gather | solution.py:172
  184.4 4.5 fusion.114
  188.9 7.0 copy-done.1
  195.9 2.2 select_reduce_fusion.2
  198.1 27.6 %pmax.7 = bf16[8192]{0:T(1024)(128)(2,1)S(1)} all-reduce(bf16[8192]{0:T(1024)(128)(2,1)S(1)} %select_reduce_fusion.2), channel_id=1, replica_groups=mesh['cells'=4,'genes'=8] {'genes'}, use_global_device_ids=true, to_apply=%region_10.11 | all-reduce | flops 8192 | bytes 32768 | tf_op jit(solution)/shard_map/pmax | solution.py:178
  225.6 7.1 select_reduce_fusion.1
  232.7 26.2 %psum.123 = f32[8192]{0:T(1024)S(1)} all-reduce(f32[8192]{0:T(1024)S(1)} %select_reduce_fusion.1), channel_id=1, replica_groups=mesh['cells'=4,'genes'=8] {'genes'}, use_global_device_ids=true, to_apply=%region_12.13 | all-reduce | flops 8192 | bytes 65536 | tf_op jit(solution)/shard_map/psum | solution.py:180
  258.9 15.5 %add_subtract_fusion = (f32[8192,320]{0,1:T(8,128)}, f32[8192,320]{0,1:T(8,128)}) fusion(f32[8192,640]{0,1:T(8,128)} %copy-done.1, f32[8192]{0:T(1024)S(1)} %log_add_fusion, f32[320]{0:T(512)S(1)} %get-tuple-element.466, f32[8192]{0:T(1024)S(1)} %copy-done.29, f32[320]{0:T(512)S(1)} %get-tuple-element.465), kind=kLoop, calls=%fused_computation.155 | loop fusion | flops 10485760 | bytes 42011136 | tf_op jit(solution)/shard_map/sub | solution.py:182
  274.4 11.9 %copy.74 = f32[8192,320]{1,0:T(8,128)} copy(f32[8192,320]{0,1:T(8,128)} %get-tuple-element.452) | data formatting | bytes 20971520 | tf_op jit(solution)/shard_map/while | solution.py:200
  286.3 11.8 %copy.75 = f32[8192,320]{1,0:T(8,128)} copy(f32[8192,320]{0,1:T(8,128)} %get-tuple-element.451) | data formatting | bytes 20971520 | tf_op jit(solution)/shard_map/while | solution.py:200
  298.1 323.2 %while.21 = (s32[]{:T(128)}, f32[4,2048]{1,0:T(4,128)S(1)}, f32[4,2048,320]{2,1,0:T(8,128)}, f32[4,2048,320]{2,1,0:T(8,128)}, f32[4,320]{1,0:T(4,128)S(1)}, /*in...) while((s32[]{:T(128)}, f32[4,2048]{1,0:T(4,128)S(1)}, ...), condition=%wide.region_20.22_spmd, body=%wide.region_13.21_spmd.sunk | while | flops 162566592 | bytes 51453508 | solution.py:200
  298.3 7.0 fusion.171
  305.3 64.6 %multiply_reduce_fusion.13 = (f32[320]{0:T(512)S(1)}, f32[2048]{0:T(1024)S(1)}, f32[320]{0:T(512)S(1)}, f32[320]{0:T(512)S(1)}, f32[320]{0:T(512)S(1)}) fusion(f32[2048,320]{1,0:T(8,128)S(1)} %get-tuple-element.570, f32[4,2048,320]{2,1,0:T(8,128)} %get-tuple-element.620, s32[]{:T(128)} %get-tuple-element.596, f32[320]{0:T(512)S(1)} %get-tuple-element.569, ...), kind=kLoop, calls=%fused_computation.91.clone.1 | loop fusion | flops 124515072 | bytes 9193796 | tf_op jit(solution)/shard_map/while/body/eval_jaxpr/transpose(jvp())/reduce_sum | solution.py:59
  370.1 8.6 fusion.172
  379.0 7.1 fusion.171
  386.1 64.6 %multiply_reduce_fusion.13 = (f32[320]{0:T(512)S(1)}, f32[2048]{0:T(1024)S(1)}, f32[320]{0:T(512)S(1)}, f32[320]{0:T(512)S(1)}, f32[320]{0:T(512)S(1)}) fusion(f32[2048,320]{1,0:T(8,128)S(1)} %get-tuple-element.570, f32[4,2048,320]{2,1,0:T(8,128)} %get-tuple-element.620, s32[]{:T(128)} %get-tuple-element.596, f32[320]{0:T(512)S(1)} %get-tuple-element.569, ...), kind=kLoop, calls=%fused_computation.91.clone.1 | loop fusion | flops 124515072 | bytes 9193796 | tf_op jit(solution)/shard_map/while/body/eval_jaxpr/transpose(jvp())/reduce_sum | solution.py:59
  450.9 8.7 fusion.172
  459.9 7.0 fusion.171
  466.9 64.6 %multiply_reduce_fusion.13 = (f32[320]{0:T(512)S(1)}, f32[2048]{0:T(1024)S(1)}, f32[320]{0:T(512)S(1)}, f32[320]{0:T(512)S(1)}, f32[320]{0:T(512)S(1)}) fusion(f32[2048,320]{1,0:T(8,128)S(1)} %get-tuple-element.570, f32[4,2048,320]{2,1,0:T(8,128)} %get-tuple-element.620, s32[]{:T(128)} %get-tuple-element.596, f32[320]{0:T(512)S(1)} %get-tuple-element.569, ...), kind=kLoop, calls=%fused_computation.91.clone.1 | loop fusion | flops 124515072 | bytes 9193796 | tf_op jit(solution)/shard_map/while/body/eval_jaxpr/transpose(jvp())/reduce_sum | solution.py:59
  531.7 8.7 fusion.172
  540.7 7.0 fusion.171
  547.7 64.6 %multiply_reduce_fusion.13 = (f32[320]{0:T(512)S(1)}, f32[2048]{0:T(1024)S(1)}, f32[320]{0:T(512)S(1)}, f32[320]{0:T(512)S(1)}, f32[320]{0:T(512)S(1)}) fusion(f32[2048,320]{1,0:T(8,128)S(1)} %get-tuple-element.570, f32[4,2048,320]{2,1,0:T(8,128)} %get-tuple-element.620, s32[]{:T(128)} %get-tuple-element.596, f32[320]{0:T(512)S(1)} %get-tuple-element.569, ...), kind=kLoop, calls=%fused_computation.91.clone.1 | loop fusion | flops 124515072 | bytes 9193796 | tf_op jit(solution)/shard_map/while/body/eval_jaxpr/transpose(jvp())/reduce_sum | solution.py:59
  612.6 8.6 fusion.172
  621.3 11.9 %copy.76 = f32[8192,320]{0,1:T(8,128)} copy(f32[8192,320]{1,0:T(8,128)} %bitcast.145) | data formatting | bytes 20971520 | tf_op jit(solution)/shard_map/reshape | solution.py:209
  633.2 5.7 reduce_sum.320
  638.9 26.4 %psum.124 = f32[8192]{0:T(1024)S(1)} all-reduce(f32[8192]{0:T(1024)S(1)} %bitcast.150), channel_id=1, replica_groups=mesh['cells'=4,'genes'=8] {'genes'}, use_global_device_ids=true, to_apply=%region_22.24 | all-reduce | flops 8192 | bytes 65536 | tf_op jit(solution)/shard_map/psum | solution.py:212
  665.3 12.6 %fusion.159 = (f32[320]{0:T(512)S(1)}, bf16[4,2048,320]{2,1,0:T(8,128)(2,1)}) fusion(f32[4,2048,320]{2,1,0:T(8,128)} %get-tuple-element.298), kind=kLoop, calls=%fused_computation.301 | loop fusion | flops 5242560 | bytes 15729920 | tf_op jit(solution)/shard_map/reduce_sum | solution.py:216
  677.9 8.2 copy.77
  686.1 9.0 fusion.158
  695.1 2.3 copy-done.5
  697.4 4.6 fusion.87
  703.0 47.4 %reduce-scatter.5.cloned.1.call-done = f32[1024,128]{1,0:T(8,128)} async-done(((f32[8192,128]{1,0:T(8,128)}), f32[1024,128]{1,0:T(8,128)}) %reduce-scatter.5.cloned.1.call-update) | async-done | bytes 524304 | tf_op jit(solution)/shard_map/reduce_scatter | solution.py:218
  751.6 37.8 %all-reduce.1 = (f32[128]{0:T(128)S(1)}, f32[128]{0:T(128)S(1)}) all-reduce(f32[128]{0:T(128)S(1)} %get-tuple-element.375, f32[128]{0:T(128)S(1)} %get-tuple-element.374), channel_id=1, replica_groups=mesh['cells'=4,'genes'=8] {'cells','genes'}, use_global_device_ids=true, to_apply=%region_27.29 | all-reduce | flops 256 | bytes 2048 | tf_op jit(solution)/shard_map/psum | solution.py:73
  790.7 2.0 multiply_add_fusion.7
  794.5 41.7 %all-reduce = (f32[128]{0:T(128)S(1)}, f32[128]{0:T(128)S(1)}, f32[129,20]{0,1:T(8,128)S(1)}) all-reduce(f32[128]{0:T(128)S(1)} %get-tuple-element.377, f32[128]{0:T(128)S(1)} %get-tuple-element.376, f32[129,20]{0,1:T(8,128)S(1)} %pad_maximum_fusion.10), channel_id=1, replica_groups=mesh['cells'=4,'genes'=8] {'cells','genes'}, use_global_device_ids=true, to_apply=%region_31.33 | all-reduce | flops 2836 | bytes 22688 | tf_op jit(solution)/shard_map/psum | solution.py:73
  837.3 8.7 fusion.86
  848.7 17.6 %all-gather.5.cloned.1.call-done = bf16[8192,128]{1,0:T(8,128)(2,1)} async-done(((bf16[1024,128]{1,0:T(8,128)(2,1)}), bf16[8192,128]{1,0:T(8,128)(2,1)}) %all-gather.5.cloned.1.call-update) | async-done | bytes 2097168 | tf_op jit(solution)/shard_map/all_gather | solution.py:248
  866.3 7.5 fusion.90
  874.4 10.0 psum.131
  886.3 105.8 %all-reduce.9.cloned.1.call-done = f32[266,128]{1,0:T(8,128)} async-done(((f32[266,128]{1,0:T(8,128)}), f32[266,128]{1,0:T(8,128)}) %all-reduce.9.cloned.1.call-update) | async-done | bytes 136208 | tf_op jit(solution)/shard_map/psum | solution.py:250
  995.5 47.6 %all-reduce.11.cloned.1.call-done = (f32[320,128]{1,0:T(8,128)}, f32[128,640]{1,0:T(8,128)}) async-done(((f32[320,128]{1,0:T(8,128)}, f32[128,640]{1,0:T(8,128)}), (f32[320,128]{1,0:T(8,128)}, f32[128,640]{1,0:T(8,128)})) %all-reduce.11.cloned.1.call-update) | async-done | bytes 491536 | tf_op jit(solution)/shard_map/psum | solution.py:249
  1049.5 29.1 %all-reduce.4 = (f32[]{:T(128)}, f32[8192]{0:T(1024)}) all-reduce(f32[]{:T(128)S(6)} %add.455, f32[8192]{0:T(1024)S(1)} %bitcast.149), channel_id=1, replica_groups=mesh['cells'=4,'genes'=8] {'genes'}, use_global_device_ids=true, to_apply=%region_41.43 | all-reduce | flops 8193 | bytes 65544 | tf_op jit(solution)/shard_map/psum | solution.py:256
  1087.4 1.9 fusion.156
  (222 shorter events, 36.5 us)
Async XLA Ops:
  7.2 61.6 %reduce-scatter.3.cloned.1.call-start = ((), (), s32[]{:S(2)}) async-start(), calls=%async_computation.2 | async-start | bytes 4718592 | tf_op jit(solution)/shard_map/reduce_scatter | solution.py:147
  15.9 52.9 %copy-start.12 = (f32[266,128]{1,0:T(8,128)S(1)}, f32[266,128]{1,0:T(8,128)}, u32[]{:S(2)}) copy-start(f32[266,128]{1,0:T(8,128)} %param.42) | copy-start | bytes 408580
  15.9 168.4 %all-gather.3.cloned.1.call-start = ((), (), s32[]{:S(2)}) async-start(), calls=%async_computation.3 | async-start | bytes 2359296 | tf_op jit(solution)/shard_map/all_gather | solution.py:172
  16.7 138.7 %copy-start.23 = (s32[1024]{0:T(1024)}, s32[1024]{0:T(1024)S(1)}, u32[]{:S(2)}) copy-start(s32[1024]{0:T(1024)S(1)} %dynamic_slice.41) | copy-start | bytes 12292
  16.9 138.6 %copy-start.37 = (f32[128]{0:T(128)}, f32[128]{0:T(128)S(1)}, u32[]{:S(2)}) copy-start(f32[128]{0:T(128)S(1)} %get-tuple-element.469) | copy-start | bytes 1540
  16.9 138.6 %copy-start.39 = (f32[128]{0:T(128)}, f32[128]{0:T(128)S(1)}, u32[]{:S(2)}) copy-start(f32[128]{0:T(128)S(1)} %get-tuple-element.472) | copy-start | bytes 1540
  16.9 138.6 %copy-start.52 = (f32[128]{0:T(128)}, f32[128]{0:T(128)S(1)}, u32[]{:S(2)}) copy-start(f32[128]{0:T(128)S(1)} %get-tuple-element.470) | copy-start | bytes 1540
  16.9 138.6 %copy-start.54 = (f32[128]{0:T(128)}, f32[128]{0:T(128)S(1)}, u32[]{:S(2)}) copy-start(f32[128]{0:T(128)S(1)} %get-tuple-element.471) | copy-start | bytes 1540
  70.3 39.9 %copy-start.6 = (f32[1024,128]{1,0:T(8,128)}, f32[1024,128]{1,0:T(8,128)S(1)}, u32[]{:S(2)}) copy-start(f32[1024,128]{1,0:T(8,128)S(1)} %get-tuple-element.477) | copy-start | bytes 1572868
  112.4 51.4 %copy-start.2 = (f32[1024,128]{1,0:T(8,128)}, f32[1024,128]{1,0:T(8,128)S(1)}, u32[]{:S(2)}) copy-start(f32[1024,128]{1,0:T(8,128)S(1)} %get-tuple-element.478) | copy-start | bytes 1572868
  155.2 595.2 %reduce-scatter.5.cloned.1.call-start = ((), (), s32[]{:S(2)}) async-start(), calls=%async_computation.4 | async-start | bytes 4718592 | tf_op jit(solution)/shard_map/reduce_scatter | solution.py:218
  225.6 33.3 %copy-start.29 = (f32[8192]{0:T(1024)S(1)}, f32[8192]{0:T(1024)}, u32[]{:S(2)}) copy-start(f32[8192]{0:T(1024)} %param.28) | copy-start | bytes 98308
  305.3 64.7 %copy-start = (f32[2048,320]{1,0:T(8,128)}, f32[2048,320]{1,0:T(8,128)S(1)}, u32[]{:S(2)}) copy-start(f32[2048,320]{1,0:T(8,128)S(1)} %get-tuple-element.570) | copy-start | bytes 7864324 | tf_op jit(solution)/shard_map/while
  386.1 64.7 %copy-start = (f32[2048,320]{1,0:T(8,128)}, f32[2048,320]{1,0:T(8,128)S(1)}, u32[]{:S(2)}) copy-start(f32[2048,320]{1,0:T(8,128)S(1)} %get-tuple-element.570) | copy-start | bytes 7864324 | tf_op jit(solution)/shard_map/while
  466.9 64.7 %copy-start = (f32[2048,320]{1,0:T(8,128)}, f32[2048,320]{1,0:T(8,128)S(1)}, u32[]{:S(2)}) copy-start(f32[2048,320]{1,0:T(8,128)S(1)} %get-tuple-element.570) | copy-start | bytes 7864324 | tf_op jit(solution)/shard_map/while
  547.7 64.7 %copy-start = (f32[2048,320]{1,0:T(8,128)}, f32[2048,320]{1,0:T(8,128)S(1)}, u32[]{:S(2)}) copy-start(f32[2048,320]{1,0:T(8,128)S(1)} %get-tuple-element.570) | copy-start | bytes 7864324 | tf_op jit(solution)/shard_map/while
  686.1 11.3 %copy-start.4 = (bf16[8192,320]{0,1:T(8,128)(2,1)S(1)}, bf16[8192,320]{0,1:T(8,128)(2,1)}, u32[]{:S(2)}) copy-start(bf16[8192,320]{0,1:T(8,128)(2,1)} %copy.77) | copy-start | bytes 15728644
  702.0 48.4 %copy-start.3 = (f32[1024,128]{1,0:T(8,128)S(1)}, f32[1024,128]{1,0:T(8,128)}, u32[]{:S(2)}) copy-start(f32[1024,128]{1,0:T(8,128)} %copy-done.2) | copy-start | bytes 1572868
  702.0 48.4 %copy-start.34 = (f32[128]{0:T(128)S(1)}, f32[128]{0:T(128)}, u32[]{:S(2)}) copy-start(f32[128]{0:T(128)} %copy-done.33) | copy-start | bytes 1540
  702.0 48.4 %copy-start.36 = (f32[128]{0:T(128)S(1)}, f32[128]{0:T(128)}, u32[]{:S(2)}) copy-start(f32[128]{0:T(128)} %copy-done.35) | copy-start | bytes 1540
  702.0 48.4 %copy-start.38 = (f32[128]{0:T(128)S(1)}, f32[128]{0:T(128)}, u32[]{:S(2)}) copy-start(f32[128]{0:T(128)} %copy-done.37) | copy-start | bytes 1540
  702.0 48.4 %copy-start.40 = (f32[128]{0:T(128)S(1)}, f32[128]{0:T(128)}, u32[]{:S(2)}) copy-start(f32[128]{0:T(128)} %copy-done.39) | copy-start | bytes 1540
  702.0 87.4 %copy-start.48 = (f32[128]{0:T(128)S(1)}, f32[128]{0:T(128)}, u32[]{:S(2)}) copy-start(f32[128]{0:T(128)} %get-tuple-element.468) | copy-start | bytes 1540
  702.0 88.7 %copy-start.13 = (f32[266,128]{1,0:T(8,128)S(1)}, f32[266,128]{1,0:T(8,128)}, u32[]{:S(2)}) copy-start(f32[266,128]{1,0:T(8,128)} %param.42) | copy-start | bytes 408580
  702.0 88.7 %copy-start.18 = (f32[1024,20]{0,1:T(8,128)S(1)}, f32[1024,20]{0,1:T(8,128)}, u32[]{:S(2)}) copy-start(f32[1024,20]{0,1:T(8,128)} %copy-done.17) | copy-start | bytes 245764
  702.0 90.7 %copy-start.7 = (f32[1024,128]{1,0:T(8,128)S(1)}, f32[1024,128]{1,0:T(8,128)}, u32[]{:S(2)}) copy-start(f32[1024,128]{1,0:T(8,128)} %copy-done.6) | copy-start | bytes 1572868
  702.0 90.6 %copy-start.45 = (f32[128]{0:T(128)S(1)}, f32[128]{0:T(128)}, u32[]{:S(2)}) copy-start(f32[128]{0:T(128)} %copy-done.44) | copy-start | bytes 1540
  702.0 90.6 %copy-start.47 = (f32[128]{0:T(128)S(1)}, f32[128]{0:T(128)}, u32[]{:S(2)}) copy-start(f32[128]{0:T(128)} %copy-done.46) | copy-start | bytes 1540
  702.1 90.6 %copy-start.53 = (f32[128]{0:T(128)S(1)}, f32[128]{0:T(128)}, u32[]{:S(2)}) copy-start(f32[128]{0:T(128)} %copy-done.52) | copy-start | bytes 1540
  702.1 90.6 %copy-start.55 = (f32[128]{0:T(128)S(1)}, f32[128]{0:T(128)}, u32[]{:S(2)}) copy-start(f32[128]{0:T(128)} %copy-done.54) | copy-start | bytes 1540
  702.1 91.2 %copy-start.28 = (f32[129,20]{0,1:T(8,128)S(1)}, f32[129,20]{0,1:T(8,128)}, u32[]{:S(2)}) copy-start(f32[129,20]{0,1:T(8,128)} %param.45) | copy-start | bytes 30964
  702.1 134.1 %copy-start.43 = (f32[128]{0:T(128)S(1)}, f32[128]{0:T(128)}, u32[]{:S(2)}) copy-start(f32[128]{0:T(128)} %get-tuple-element.467) | copy-start | bytes 1540
  702.1 164.1 %all-gather.5.cloned.1.call-start = ((), (), s32[]{:S(2)}) async-start(), calls=%async_computation.5 | async-start | bytes 2359296 | tf_op jit(solution)/shard_map/all_gather | solution.py:248
  789.4 95.6 %copy-start.42 = (f32[128]{0:T(128)}, f32[128]{0:T(128)S(1)}, u32[]{:S(2)}) copy-start(f32[128]{0:T(128)S(1)} %get-tuple-element.411) | copy-start | bytes 1540
  789.4 95.6 %copy-start.50 = (f32[128]{0:T(128)}, f32[128]{0:T(128)S(1)}, u32[]{:S(2)}) copy-start(f32[128]{0:T(128)S(1)} %get-tuple-element.412) | copy-start | bytes 1540
  836.1 48.9 %copy-start.41 = (f32[128]{0:T(128)}, f32[128]{0:T(128)S(1)}, u32[]{:S(2)}) copy-start(f32[128]{0:T(128)S(1)} %get-tuple-element.408) | copy-start | bytes 1540
  836.2 48.9 %copy-start.51 = (f32[128]{0:T(128)}, f32[128]{0:T(128)S(1)}, u32[]{:S(2)}) copy-start(f32[128]{0:T(128)S(1)} %get-tuple-element.409) | copy-start | bytes 1540
  836.2 49.5 %copy-start.25 = (f32[129,20]{0,1:T(8,128)}, f32[129,20]{0,1:T(8,128)S(1)}, u32[]{:S(2)}) copy-start(f32[129,20]{0,1:T(8,128)S(1)} %get-tuple-element.410) | copy-start | bytes 30964
  837.1 154.9 %all-reduce.9.cloned.1.call-start = ((), (), s32[]{:S(2)}) async-start(), calls=%async_computation.6 | async-start | bytes 278528 | tf_op jit(solution)/shard_map/psum | solution.py:250
  848.6 25.2 %copy-start.9 = (f32[2,128,320]{1,2,0:T(8,128)S(1)}, f32[2,128,320]{1,2,0:T(8,128)}, u32[]{:S(2)}) copy-start(f32[2,128,320]{1,2,0:T(8,128)} %param.36) | copy-start | bytes 983044
  848.6 25.4 %copy-start.19 = (f32[2,128,320]{1,2,0:T(8,128)S(1)}, f32[2,128,320]{1,2,0:T(8,128)}, u32[]{:S(2)}) copy-start(f32[2,128,320]{1,2,0:T(8,128)} %param.37) | copy-start | bytes 983044
  848.6 25.5 %copy-start.20 = (f32[2,128,320]{1,2,0:T(8,128)S(1)}, f32[2,128,320]{1,2,0:T(8,128)}, u32[]{:S(2)}) copy-start(f32[2,128,320]{1,2,0:T(8,128)} %param.38) | copy-start | bytes 983044
  848.6 194.5 %all-reduce.11.cloned.1.call-start = ((), (), s32[]{:S(2)}) async-start(), calls=%async_computation.7 | async-start | bytes 983040 | tf_op jit(solution)/shard_map/psum | solution.py:249
  884.4 194.9 %copy-start.26 = (f32[3,320]{1,0:T(4,128)}, f32[3,320]{1,0:T(4,128)S(1)}, u32[]{:S(2)}) copy-start(f32[3,320]{1,0:T(4,128)S(1)} %psum.131) | copy-start | bytes 11524
  1045.9 41.5 %copy-start.10 = (f32[320,128]{1,0:T(8,128)S(1)}, f32[320,128]{1,0:T(8,128)}, u32[]{:S(2)}) copy-start(f32[320,128]{1,0:T(8,128)} %get-tuple-element.419) | copy-start | bytes 491524
  1045.9 41.5 %copy-start.11 = (f32[320,128]{1,0:T(8,128)S(1)}, f32[320,128]{1,0:T(8,128)}, u32[]{:S(2)}) copy-start(f32[320,128]{1,0:T(8,128)} %param.33) | copy-start | bytes 491524
  1079.3 11.2 %copy-start.16 = (f32[266,128]{1,0:T(8,128)S(1)}, f32[266,128]{1,0:T(8,128)}, u32[]{:S(2)}) copy-start(f32[266,128]{1,0:T(8,128)} %all-reduce.9.cloned.1.call-done) | copy-start | bytes 408580
  1079.7 10.9 copy-start.21
  (17 other events, 79.8 us)
Sparse Core Ops, SparseCore 0:
  16.1 52.6 reduce-scatter.2
  155.3 29.0 all-gather.2
  702.2 48.0 reduce-scatter.4
  837.2 29.0 all-gather.4
  872.2 119.7 all-reduce.8
  995.5 47.5 all-reduce.10
where the time goes:
time: 1110 us; the launch traced here: 1100 us
  other arithmetic  396 us (36%)
  waiting for transfers between devices  291 us (26%)
  blocking collectives  278 us (25%)
  local copies, waits for them, and re-layouts  69.4 us (6%)
  matrix products  42.9 us (4%)
  between operations  21.7 us (2%)
    reduce_sum x4, other arithmetic, zinb_loglik(): drop_term = -drop_logit + dispersion * (log_disp_eps - log_both)  259 us
    psum x4, blocking collectives, wide_sum(): return lax.psum((values[0], values[1]), ('cells', 'genes'))  159 us
    psum x1, waiting for transfers between devices, per_device(): lax.psum((grad_small, grad_head), ('cells', 'genes'))  106 us
    reduce_scatter x1, waiting for transfers between devices, per_device(): lax.psum_scatter(jnp.dot(cell_rows, enc_low, preferred_element_type=jnp.f...  51.9 us
    psum x1, waiting for transfers between devices, per_device(): lax.psum((grad_enc, grad_dec, grad_gene), 'cells')  47.6 us
    reduce_scatter x1, waiting for transfers between devices, per_device(): lax.psum_scatter(plain_back(cell_rows, dec_cat), 'genes', scatter_dimensi...  47.4 us
    dynamic_update_slice x4, other arithmetic, per_device(): lax.map(block_grad, (counts.reshape(count_blocks, block_rows, local_genes...  34.7 us
    psum x1, blocking collectives, per_device(): gene_square = lax.psum(gene_square, 'genes')  29.1 us
  transfers between devices with their start and end apart: 6, of which 6 were waited for; matrix products, arithmetic and copies ran while one was open for 3% of the time, Pallas kernels for 0%

commit v1 on v0

--- a/solution.py
+++ b/solution.py
@@ -70,7 +70,7 @@
 
 
 def wide_sum(values):
-    return lax.psum((values[0], values[1]), ("cells", "genes"))
+    return lax.psum(lax.psum((values[0], values[1]), axis_name="genes"), "cells")
 
 
 def norm_forward(pre_act, gain_row, shift_row, cell_total):

time: 1110 us -> 1030 us (0.928)
  blocking collectives: 278 us -> 240 us
  waiting for transfers between devices: 291 us -> 254 us
    psum x5 -> x9, blocking collectives: 169 us -> 131 us  [the longest x4 54.8 us: wide_sum(): lax.psum((values[0], values[1]), axis_name='genes')]
    psum x1, waiting for transfers between devices: 106 us -> 75.3 us  [per_device(): lax.psum((grad_small, grad_head), ('cells', 'genes'))]
where the time goes in v1:
time: 1030 us
  other arithmetic  396 us (38%)
  waiting for transfers between devices  254 us (25%)
  blocking collectives  240 us (23%)
  local copies, waits for them, and re-layouts  69.4 us (7%)
  matrix products  43.1 us (4%)
  between operations  22 us (2%)
    reduce_sum x4, other arithmetic, zinb_loglik(): drop_term = -drop_logit + dispersion * (log_disp_eps - log_both)  259 us
    psum x1, waiting for transfers between devices, per_device(): lax.psum((grad_small, grad_head), ('cells', 'genes'))  75.3 us
    psum x4, blocking collectives, wide_sum(): lax.psum((values[0], values[1]), axis_name='genes')  54.8 us
    reduce_scatter x1, waiting for transfers between devices, per_device(): lax.psum_scatter(jnp.dot(cell_rows, enc_low, preferred_element_type=jnp.f...  51.9 us
    psum x1, waiting for transfers between devices, per_device(): lax.psum((grad_enc, grad_dec, grad_gene), 'cells')  47.6 us
    reduce_scatter x1, waiting for transfers between devices, per_device(): lax.psum_scatter(plain_back(cell_rows, dec_cat), 'genes', scatter_dimensi...  47.3 us
    psum x1, blocking collectives, per_device(): lax.psum((grad_small, grad_head), ('cells', 'genes'))  40.3 us
    psum x4, blocking collectives, wide_sum(): lax.psum(lax.psum((values[0], values[1]), axis_name='genes'), 'cells')  35.7 us
  transfers between devices with their start and end apart: 6, of which 6 were waited for; matrix products, arithmetic and copies ran while one was open for 3% of the time, Pallas kernels for 0%

profile of v1, /device:TPU:0, one launch (start us, length us, event | category | flops | bytes accessed | tf_op | source)
XLA Modules:
  0.0 1025.7 jit_solution(7060303458582121681)
XLA Ops:
  7.2 8.7 fusion.89
  16.9 51.9 %reduce-scatter.3.cloned.1.call-done = f32[1024,128]{1,0:T(8,128)} async-done(((f32[8192,128]{1,0:T(8,128)}), f32[1024,128]{1,0:T(8,128)}) %reduce-scatter.3.cloned.1.call-update) | async-done | bytes 524304 | tf_op jit(solution)/shard_map/reduce_scatter | solution.py:147
  70.3 13.8 %all-reduce.4 = (f32[128]{0:T(128)S(1)}, f32[128]{0:T(128)S(1)}) all-reduce(f32[128]{0:T(128)S(1)} %get-tuple-element.381, f32[128]{0:T(128)S(1)} %get-tuple-element.380), channel_id=1, replica_groups=mesh['cells'=4,'genes'=8] {'genes'}, use_global_device_ids=true, to_apply=%region_2.0 | all-reduce | flops 256 | bytes 2048 | tf_op jit(solution)/shard_map/psum | solution.py:73
  84.1 9.9 all-reduce.8
  98.2 13.6 %all-reduce.3 = (f32[128]{0:T(128)S(1)}, f32[128]{0:T(128)S(1)}) all-reduce(f32[128]{0:T(128)S(1)} %get-tuple-element.379, f32[128]{0:T(128)S(1)} %get-tuple-element.378), channel_id=1, replica_groups=mesh['cells'=4,'genes'=8] {'genes'}, use_global_device_ids=true, to_apply=%region_8.9 | all-reduce | flops 256 | bytes 2048 | tf_op jit(solution)/shard_map/psum | solution.py:73
  111.8 7.9 all-reduce.7
  121.8 8.2 copy.60
  130.1 17.6 %all-gather.3.cloned.1.call-done = bf16[8192,128]{1,0:T(8,128)(2,1)} async-done(((bf16[1024,128]{1,0:T(8,128)(2,1)}), bf16[8192,128]{1,0:T(8,128)(2,1)}) %all-gather.3.cloned.1.call-update) | async-done | bytes 2097168 | tf_op jit(solution)/shard_map/all_gather | solution.py:172
  147.7 4.5 fusion.114
  152.2 7.0 copy-done.1
  161.4 27.6 %pmax.7 = bf16[8192]{0:T(1024)(128)(2,1)S(1)} all-reduce(bf16[8192]{0:T(1024)(128)(2,1)S(1)} %select_reduce_fusion.2), channel_id=1, replica_groups=mesh['cells'=4,'genes'=8] {'genes'}, use_global_device_ids=true, to_apply=%region_14.15 | all-reduce | flops 8192 | bytes 32768 | tf_op jit(solution)/shard_map/pmax | solution.py:178
  189.0 7.1 select_reduce_fusion.1
  196.0 26.1 %psum.183 = f32[8192]{0:T(1024)S(1)} all-reduce(f32[8192]{0:T(1024)S(1)} %select_reduce_fusion.1), channel_id=1, replica_groups=mesh['cells'=4,'genes'=8] {'genes'}, use_global_device_ids=true, to_apply=%region_16.17 | all-reduce | flops 8192 | bytes 65536 | tf_op jit(solution)/shard_map/psum | solution.py:180
  222.2 15.5 %add_subtract_fusion = (f32[8192,320]{0,1:T(8,128)}, f32[8192,320]{0,1:T(8,128)}) fusion(f32[8192,640]{0,1:T(8,128)} %copy-done.1, f32[8192]{0:T(1024)S(1)} %log_add_fusion, f32[320]{0:T(512)S(1)} %get-tuple-element.474, f32[8192]{0:T(1024)S(1)} %copy-done.28, f32[320]{0:T(512)S(1)} %get-tuple-element.473), kind=kLoop, calls=%fused_computation.155 | loop fusion | flops 10485760 | bytes 42011136 | tf_op jit(solution)/shard_map/sub | solution.py:182
  237.7 11.9 %copy.74 = f32[8192,320]{1,0:T(8,128)} copy(f32[8192,320]{0,1:T(8,128)} %get-tuple-element.460) | data formatting | bytes 20971520 | tf_op jit(solution)/shard_map/while | solution.py:200
  249.6 11.8 %copy.75 = f32[8192,320]{1,0:T(8,128)} copy(f32[8192,320]{0,1:T(8,128)} %get-tuple-element.459) | data formatting | bytes 20971520 | tf_op jit(solution)/shard_map/while | solution.py:200
  261.4 323.2 %while.21 = (s32[]{:T(128)}, f32[4,2048]{1,0:T(4,128)S(1)}, f32[4,2048,320]{2,1,0:T(8,128)}, f32[4,2048,320]{2,1,0:T(8,128)}, f32[4,320]{1,0:T(4,128)S(1)}, /*in...) while((s32[]{:T(128)}, f32[4,2048]{1,0:T(4,128)S(1)}, ...), condition=%wide.region_24.26_spmd, body=%wide.region_17.25_spmd.sunk | while | flops 162566592 | bytes 51453508 | solution.py:200
  261.5 7.0 fusion.171
  268.6 64.6 %multiply_reduce_fusion.13 = (f32[320]{0:T(512)S(1)}, f32[2048]{0:T(1024)S(1)}, f32[320]{0:T(512)S(1)}, f32[320]{0:T(512)S(1)}, f32[320]{0:T(512)S(1)}) fusion(f32[2048,320]{1,0:T(8,128)S(1)} %get-tuple-element.578, f32[4,2048,320]{2,1,0:T(8,128)} %get-tuple-element.628, s32[]{:T(128)} %get-tuple-element.604, f32[320]{0:T(512)S(1)} %get-tuple-element.577, ...), kind=kLoop, calls=%fused_computation.91.clone.1 | loop fusion | flops 124515072 | bytes 9193796 | tf_op jit(solution)/shard_map/while/body/eval_jaxpr/transpose(jvp())/reduce_sum | solution.py:59
  333.4 8.6 fusion.172
  342.3 7.1 fusion.171
  349.3 64.6 %multiply_reduce_fusion.13 = (f32[320]{0:T(512)S(1)}, f32[2048]{0:T(1024)S(1)}, f32[320]{0:T(512)S(1)}, f32[320]{0:T(512)S(1)}, f32[320]{0:T(512)S(1)}) fusion(f32[2048,320]{1,0:T(8,128)S(1)} %get-tuple-element.578, f32[4,2048,320]{2,1,0:T(8,128)} %get-tuple-element.628, s32[]{:T(128)} %get-tuple-element.604, f32[320]{0:T(512)S(1)} %get-tuple-element.577, ...), kind=kLoop, calls=%fused_computation.91.clone.1 | loop fusion | flops 124515072 | bytes 9193796 | tf_op jit(solution)/shard_map/while/body/eval_jaxpr/transpose(jvp())/reduce_sum | solution.py:59
  414.2 8.7 fusion.172
  423.1 7.0 fusion.171
  430.2 64.6 %multiply_reduce_fusion.13 = (f32[320]{0:T(512)S(1)}, f32[2048]{0:T(1024)S(1)}, f32[320]{0:T(512)S(1)}, f32[320]{0:T(512)S(1)}, f32[320]{0:T(512)S(1)}) fusion(f32[2048,320]{1,0:T(8,128)S(1)} %get-tuple-element.578, f32[4,2048,320]{2,1,0:T(8,128)} %get-tuple-element.628, s32[]{:T(128)} %get-tuple-element.604, f32[320]{0:T(512)S(1)} %get-tuple-element.577, ...), kind=kLoop, calls=%fused_computation.91.clone.1 | loop fusion | flops 124515072 | bytes 9193796 | tf_op jit(solution)/shard_map/while/body/eval_jaxpr/transpose(jvp())/reduce_sum | solution.py:59
  495.0 8.7 fusion.172
  504.0 7.0 fusion.171
  511.0 64.6 %multiply_reduce_fusion.13 = (f32[320]{0:T(512)S(1)}, f32[2048]{0:T(1024)S(1)}, f32[320]{0:T(512)S(1)}, f32[320]{0:T(512)S(1)}, f32[320]{0:T(512)S(1)}) fusion(f32[2048,320]{1,0:T(8,128)S(1)} %get-tuple-element.578, f32[4,2048,320]{2,1,0:T(8,128)} %get-tuple-element.628, s32[]{:T(128)} %get-tuple-element.604, f32[320]{0:T(512)S(1)} %get-tuple-element.577, ...), kind=kLoop, calls=%fused_computation.91.clone.1 | loop fusion | flops 124515072 | bytes 9193796 | tf_op jit(solution)/shard_map/while/body/eval_jaxpr/transpose(jvp())/reduce_sum | solution.py:59
  575.8 8.6 fusion.172
  584.6 11.9 %copy.76 = f32[8192,320]{0,1:T(8,128)} copy(f32[8192,320]{1,0:T(8,128)} %bitcast.145) | data formatting | bytes 20971520 | tf_op jit(solution)/shard_map/reshape | solution.py:209
  596.5 5.7 reduce_sum.320
  602.2 26.2 %psum.184 = f32[8192]{0:T(1024)S(1)} all-reduce(f32[8192]{0:T(1024)S(1)} %bitcast.150), channel_id=1, replica_groups=mesh['cells'=4,'genes'=8] {'genes'}, use_global_device_ids=true, to_apply=%region_26.28 | all-reduce | flops 8192 | bytes 65536 | tf_op jit(solution)/shard_map/psum | solution.py:212
  628.4 12.6 %fusion.159 = (f32[320]{0:T(512)S(1)}, bf16[4,2048,320]{2,1,0:T(8,128)(2,1)}) fusion(f32[4,2048,320]{2,1,0:T(8,128)} %get-tuple-element.298), kind=kLoop, calls=%fused_computation.301 | loop fusion | flops 5242560 | bytes 15729920 | tf_op jit(solution)/shard_map/reduce_sum | solution.py:216
  640.9 8.2 copy.77
  649.2 9.0 fusion.158
  660.5 4.6 fusion.87
  666.2 47.3 %reduce-scatter.5.cloned.1.call-done = f32[1024,128]{1,0:T(8,128)} async-done(((f32[8192,128]{1,0:T(8,128)}), f32[1024,128]{1,0:T(8,128)}) %reduce-scatter.5.cloned.1.call-update) | async-done | bytes 524304 | tf_op jit(solution)/shard_map/reduce_scatter | solution.py:218
  714.7 13.9 %all-reduce.2 = (f32[128]{0:T(128)S(1)}, f32[128]{0:T(128)S(1)}) all-reduce(f32[128]{0:T(128)S(1)} %get-tuple-element.375, f32[128]{0:T(128)S(1)} %get-tuple-element.374), channel_id=1, replica_groups=mesh['cells'=4,'genes'=8] {'genes'}, use_global_device_ids=true, to_apply=%region_32.34 | all-reduce | flops 256 | bytes 2048 | tf_op jit(solution)/shard_map/psum | solution.py:73
  728.6 9.9 all-reduce.6
  742.9 13.6 %all-reduce.1 = (f32[128]{0:T(128)S(1)}, f32[128]{0:T(128)S(1)}) all-reduce(f32[128]{0:T(128)S(1)} %get-tuple-element.377, f32[128]{0:T(128)S(1)} %get-tuple-element.376), channel_id=1, replica_groups=mesh['cells'=4,'genes'=8] {'genes'}, use_global_device_ids=true, to_apply=%region_38.40 | all-reduce | flops 256 | bytes 2048 | tf_op jit(solution)/shard_map/psum | solution.py:73
  756.5 8.1 all-reduce.5
  766.4 8.9 fusion.86
  777.9 14.2 %all-gather.5.cloned.1.call-done = bf16[8192,128]{1,0:T(8,128)(2,1)} async-done(((bf16[1024,128]{1,0:T(8,128)(2,1)}), bf16[8192,128]{1,0:T(8,128)(2,1)}) %all-gather.5.cloned.1.call-update) | async-done | bytes 2097168 | tf_op jit(solution)/shard_map/all_gather | solution.py:248
  792.1 7.5 fusion.90
  801.0 40.3 %psum.198 = f32[129,20]{0,1:T(8,128)S(1)} all-reduce(f32[129,20]{0,1:T(8,128)S(1)} %pad_maximum_fusion.10), channel_id=1, replica_groups=mesh['cells'=4,'genes'=8] {'cells','genes'}, use_global_device_ids=true, to_apply=%region_53.55 | all-reduce | flops 2580 | bytes 20640 | tf_op jit(solution)/shard_map/psum | solution.py:250
  842.5 75.3 %all-reduce.13.cloned.1.call-done = f32[266,128]{1,0:T(8,128)} async-done(((f32[266,128]{1,0:T(8,128)}), f32[266,128]{1,0:T(8,128)}) %all-reduce.13.cloned.1.call-update) | async-done | bytes 136208 | tf_op jit(solution)/shard_map/psum | solution.py:250
  921.4 47.6 %all-reduce.15.cloned.1.call-done = (f32[320,128]{1,0:T(8,128)}, f32[128,640]{1,0:T(8,128)}) async-done(((f32[320,128]{1,0:T(8,128)}, f32[128,640]{1,0:T(8,128)}), (f32[320,128]{1,0:T(8,128)}, f32[128,640]{1,0:T(8,128)})) %all-reduce.15.cloned.1.call-update) | async-done | bytes 491536 | tf_op jit(solution)/shard_map/psum | solution.py:249
  975.4 29.1 %all-reduce = (f32[]{:T(128)}, f32[8192]{0:T(1024)}) all-reduce(f32[]{:T(128)S(6)} %add.471, f32[8192]{0:T(1024)S(1)} %bitcast.149), channel_id=1, replica_groups=mesh['cells'=4,'genes'=8] {'genes'}, use_global_device_ids=true, to_apply=%region_49.51 | all-reduce | flops 8193 | bytes 65544 | tf_op jit(solution)/shard_map/psum | solution.py:256
  (226 shorter events, 45.3 us)
Async XLA Ops:
  7.2 61.6 %reduce-scatter.3.cloned.1.call-start = ((), (), s32[]{:S(2)}) async-start(), calls=%async_computation.2 | async-start | bytes 4718592 | tf_op jit(solution)/shard_map/reduce_scatter | solution.py:147
  15.9 52.9 %copy-start.12 = (f32[266,128]{1,0:T(8,128)S(1)}, f32[266,128]{1,0:T(8,128)}, u32[]{:S(2)}) copy-start(f32[266,128]{1,0:T(8,128)} %param.42) | copy-start | bytes 408580
  15.9 131.7 %all-gather.3.cloned.1.call-start = ((), (), s32[]{:S(2)}) async-start(), calls=%async_computation.3 | async-start | bytes 2359296 | tf_op jit(solution)/shard_map/all_gather | solution.py:172
  16.7 104.9 %copy-start.24 = (s32[1024]{0:T(1024)}, s32[1024]{0:T(1024)S(1)}, u32[]{:S(2)}) copy-start(s32[1024]{0:T(1024)S(1)} %dynamic_slice.41) | copy-start | bytes 12292
  16.9 104.8 %copy-start.37 = (f32[128]{0:T(128)}, f32[128]{0:T(128)S(1)}, u32[]{:S(2)}) copy-start(f32[128]{0:T(128)S(1)} %get-tuple-element.477) | copy-start | bytes 1540
  16.9 104.8 %copy-start.39 = (f32[128]{0:T(128)}, f32[128]{0:T(128)S(1)}, u32[]{:S(2)}) copy-start(f32[128]{0:T(128)S(1)} %get-tuple-element.480) | copy-start | bytes 1540
  16.9 104.8 %copy-start.52 = (f32[128]{0:T(128)}, f32[128]{0:T(128)S(1)}, u32[]{:S(2)}) copy-start(f32[128]{0:T(128)S(1)} %get-tuple-element.478) | copy-start | bytes 1540
  16.9 104.8 %copy-start.54 = (f32[128]{0:T(128)}, f32[128]{0:T(128)S(1)}, u32[]{:S(2)}) copy-start(f32[128]{0:T(128)S(1)} %get-tuple-element.479) | copy-start | bytes 1540
  70.3 25.8 %copy-start.6 = (f32[1024,128]{1,0:T(8,128)}, f32[1024,128]{1,0:T(8,128)S(1)}, u32[]{:S(2)}) copy-start(f32[1024,128]{1,0:T(8,128)S(1)} %get-tuple-element.485) | copy-start | bytes 1572868
  98.2 31.8 %copy-start.2 = (f32[1024,128]{1,0:T(8,128)}, f32[1024,128]{1,0:T(8,128)S(1)}, u32[]{:S(2)}) copy-start(f32[1024,128]{1,0:T(8,128)S(1)} %get-tuple-element.486) | copy-start | bytes 1572868
  121.1 592.4 %reduce-scatter.5.cloned.1.call-start = ((), (), s32[]{:S(2)}) async-start(), calls=%async_computation.4 | async-start | bytes 4718592 | tf_op jit(solution)/shard_map/reduce_scatter | solution.py:218
  189.0 33.2 %copy-start.28 = (f32[8192]{0:T(1024)S(1)}, f32[8192]{0:T(1024)}, u32[]{:S(2)}) copy-start(f32[8192]{0:T(1024)} %param.28) | copy-start | bytes 98308
  268.6 64.7 %copy-start = (f32[2048,320]{1,0:T(8,128)}, f32[2048,320]{1,0:T(8,128)S(1)}, u32[]{:S(2)}) copy-start(f32[2048,320]{1,0:T(8,128)S(1)} %get-tuple-element.578) | copy-start | bytes 7864324 | tf_op jit(solution)/shard_map/while
  349.3 64.7 %copy-start = (f32[2048,320]{1,0:T(8,128)}, f32[2048,320]{1,0:T(8,128)S(1)}, u32[]{:S(2)}) copy-start(f32[2048,320]{1,0:T(8,128)S(1)} %get-tuple-element.578) | copy-start | bytes 7864324 | tf_op jit(solution)/shard_map/while
  430.2 64.7 %copy-start = (f32[2048,320]{1,0:T(8,128)}, f32[2048,320]{1,0:T(8,128)S(1)}, u32[]{:S(2)}) copy-start(f32[2048,320]{1,0:T(8,128)S(1)} %get-tuple-element.578) | copy-start | bytes 7864324 | tf_op jit(solution)/shard_map/while
  511.0 64.7 %copy-start = (f32[2048,320]{1,0:T(8,128)}, f32[2048,320]{1,0:T(8,128)S(1)}, u32[]{:S(2)}) copy-start(f32[2048,320]{1,0:T(8,128)S(1)} %get-tuple-element.578) | copy-start | bytes 7864324 | tf_op jit(solution)/shard_map/while
  649.2 11.3 %copy-start.4 = (bf16[8192,320]{0,1:T(8,128)(2,1)S(1)}, bf16[8192,320]{0,1:T(8,128)(2,1)}, u32[]{:S(2)}) copy-start(bf16[8192,320]{0,1:T(8,128)(2,1)} %copy.77) | copy-start | bytes 15728644
  665.0 48.5 %copy-start.3 = (f32[1024,128]{1,0:T(8,128)S(1)}, f32[1024,128]{1,0:T(8,128)}, u32[]{:S(2)}) copy-start(f32[1024,128]{1,0:T(8,128)} %copy-done.2) | copy-start | bytes 1572868
  665.0 48.5 %copy-start.34 = (f32[128]{0:T(128)S(1)}, f32[128]{0:T(128)}, u32[]{:S(2)}) copy-start(f32[128]{0:T(128)} %copy-done.33) | copy-start | bytes 1540
  665.0 48.5 %copy-start.36 = (f32[128]{0:T(128)S(1)}, f32[128]{0:T(128)}, u32[]{:S(2)}) copy-start(f32[128]{0:T(128)} %copy-done.35) | copy-start | bytes 1540
  665.1 48.5 %copy-start.38 = (f32[128]{0:T(128)S(1)}, f32[128]{0:T(128)}, u32[]{:S(2)}) copy-start(f32[128]{0:T(128)} %copy-done.37) | copy-start | bytes 1540
  665.1 48.5 %copy-start.40 = (f32[128]{0:T(128)S(1)}, f32[128]{0:T(128)}, u32[]{:S(2)}) copy-start(f32[128]{0:T(128)} %copy-done.39) | copy-start | bytes 1540
  665.1 73.4 %copy-start.48 = (f32[128]{0:T(128)S(1)}, f32[128]{0:T(128)}, u32[]{:S(2)}) copy-start(f32[128]{0:T(128)} %get-tuple-element.476) | copy-start | bytes 1540
  665.1 74.7 %copy-start.13 = (f32[266,128]{1,0:T(8,128)S(1)}, f32[266,128]{1,0:T(8,128)}, u32[]{:S(2)}) copy-start(f32[266,128]{1,0:T(8,128)} %param.42) | copy-start | bytes 408580
  665.1 74.7 %copy-start.18 = (f32[1024,20]{0,1:T(8,128)S(1)}, f32[1024,20]{0,1:T(8,128)}, u32[]{:S(2)}) copy-start(f32[1024,20]{0,1:T(8,128)} %copy-done.17) | copy-start | bytes 245764
  665.1 76.7 %copy-start.7 = (f32[1024,128]{1,0:T(8,128)S(1)}, f32[1024,128]{1,0:T(8,128)}, u32[]{:S(2)}) copy-start(f32[1024,128]{1,0:T(8,128)} %copy-done.6) | copy-start | bytes 1572868
  665.1 76.7 %copy-start.27 = (f32[129,20]{0,1:T(8,128)S(1)}, f32[129,20]{0,1:T(8,128)}, u32[]{:S(2)}) copy-start(f32[129,20]{0,1:T(8,128)} %param.45) | copy-start | bytes 30964
  665.1 76.7 %copy-start.45 = (f32[128]{0:T(128)S(1)}, f32[128]{0:T(128)}, u32[]{:S(2)}) copy-start(f32[128]{0:T(128)} %copy-done.44) | copy-start | bytes 1540
  665.1 76.7 %copy-start.47 = (f32[128]{0:T(128)S(1)}, f32[128]{0:T(128)}, u32[]{:S(2)}) copy-start(f32[128]{0:T(128)} %copy-done.46) | copy-start | bytes 1540
  665.2 76.7 %copy-start.53 = (f32[128]{0:T(128)S(1)}, f32[128]{0:T(128)}, u32[]{:S(2)}) copy-start(f32[128]{0:T(128)} %copy-done.52) | copy-start | bytes 1540
  665.2 76.7 %copy-start.55 = (f32[128]{0:T(128)S(1)}, f32[128]{0:T(128)}, u32[]{:S(2)}) copy-start(f32[128]{0:T(128)} %copy-done.54) | copy-start | bytes 1540
  665.2 99.4 %copy-start.43 = (f32[128]{0:T(128)S(1)}, f32[128]{0:T(128)}, u32[]{:S(2)}) copy-start(f32[128]{0:T(128)} %get-tuple-element.475) | copy-start | bytes 1540
  665.2 126.9 %all-gather.5.cloned.1.call-start = ((), (), s32[]{:S(2)}) async-start(), calls=%async_computation.5 | async-start | bytes 2359296 | tf_op jit(solution)/shard_map/all_gather | solution.py:248
  666.2 99.6 %copy-start.9 = (f32[2,128,320]{1,2,0:T(8,128)S(1)}, f32[2,128,320]{1,2,0:T(8,128)}, u32[]{:S(2)}) copy-start(f32[2,128,320]{1,2,0:T(8,128)} %param.36) | copy-start | bytes 983044
  714.7 51.3 %copy-start.19 = (f32[2,128,320]{1,2,0:T(8,128)S(1)}, f32[2,128,320]{1,2,0:T(8,128)}, u32[]{:S(2)}) copy-start(f32[2,128,320]{1,2,0:T(8,128)} %param.37) | copy-start | bytes 983044
  738.5 61.9 %copy-start.42 = (f32[128]{0:T(128)}, f32[128]{0:T(128)S(1)}, u32[]{:S(2)}) copy-start(f32[128]{0:T(128)S(1)} %get-tuple-element.421) | copy-start | bytes 1540
  738.5 61.9 %copy-start.50 = (f32[128]{0:T(128)}, f32[128]{0:T(128)S(1)}, u32[]{:S(2)}) copy-start(f32[128]{0:T(128)S(1)} %get-tuple-element.422) | copy-start | bytes 1540
  738.5 27.6 %copy-start.20 = (f32[2,128,320]{1,2,0:T(8,128)S(1)}, f32[2,128,320]{1,2,0:T(8,128)}, u32[]{:S(2)}) copy-start(f32[2,128,320]{1,2,0:T(8,128)} %param.38) | copy-start | bytes 983044
  764.6 35.8 %copy-start.41 = (f32[128]{0:T(128)}, f32[128]{0:T(128)S(1)}, u32[]{:S(2)}) copy-start(f32[128]{0:T(128)S(1)} %get-tuple-element.418) | copy-start | bytes 1540
  764.6 35.8 %copy-start.51 = (f32[128]{0:T(128)}, f32[128]{0:T(128)S(1)}, u32[]{:S(2)}) copy-start(f32[128]{0:T(128)S(1)} %get-tuple-element.419) | copy-start | bytes 1540
  764.6 76.7 %copy-start.29 = (f32[3,320]{1,0:T(4,128)}, f32[3,320]{1,0:T(4,128)S(1)}, u32[]{:S(2)}) copy-start(f32[3,320]{1,0:T(4,128)S(1)} %get-tuple-element.420) | copy-start | bytes 11524
  765.5 152.4 %all-reduce.13.cloned.1.call-start = ((), (), s32[]{:S(2)}) async-start(), calls=%async_computation.6 | async-start | bytes 278528 | tf_op jit(solution)/shard_map/psum | solution.py:250
  777.9 191.1 %all-reduce.15.cloned.1.call-start = ((), (), s32[]{:S(2)}) async-start(), calls=%async_computation.7 | async-start | bytes 983040 | tf_op jit(solution)/shard_map/psum | solution.py:249
  841.3 163.9 %copy-start.21 = (f32[129,20]{0,1:T(8,128)}, f32[129,20]{0,1:T(8,128)S(1)}, u32[]{:S(2)}) copy-start(f32[129,20]{0,1:T(8,128)S(1)} %psum.198) | copy-start | bytes 30964
  971.8 41.5 %copy-start.10 = (f32[320,128]{1,0:T(8,128)S(1)}, f32[320,128]{1,0:T(8,128)}, u32[]{:S(2)}) copy-start(f32[320,128]{1,0:T(8,128)} %get-tuple-element.427) | copy-start | bytes 491524
  971.8 41.5 %copy-start.11 = (f32[320,128]{1,0:T(8,128)S(1)}, f32[320,128]{1,0:T(8,128)}, u32[]{:S(2)}) copy-start(f32[320,128]{1,0:T(8,128)} %param.33) | copy-start | bytes 491524
  1005.2 11.2 %copy-start.16 = (f32[266,128]{1,0:T(8,128)S(1)}, f32[266,128]{1,0:T(8,128)}, u32[]{:S(2)}) copy-start(f32[266,128]{1,0:T(8,128)} %all-reduce.13.cloned.1.call-done) | copy-start | bytes 408580
  1005.6 10.9 %copy-start.22 = (f32[266,128]{1,0:T(8,128)S(1)}, f32[266,128]{1,0:T(8,128)}, u32[]{:S(2)}) copy-start(f32[266,128]{1,0:T(8,128)} %param.43) | copy-start | bytes 408580
  (17 other events, 80.3 us)
Sparse Core Ops, SparseCore 0:
  16.1 52.6 reduce-scatter.2
  121.2 26.4 all-gather.2
  665.3 48.1 reduce-scatter.4
  765.6 26.4 all-gather.4
  798.1 119.7 all-reduce.12
  921.4 47.5 all-reduce.14
